TPU v7x, 256 devices: a whole 4x4x8 slice. The times are simulated.
256 devices in a mesh: row: 32 (over z, x), col: 8 (over y, core).
Axes of the slice: x: 4, y: 4, z: 8, core: 2. Of those that a mesh axis runs over, the one named last changes fastest.
Arguments:
- eigvecs: float32 [98304, 2048], P('row', 'col'), may hold values from -6 to 6
- reflectors: float32 [98304, 2048], P('row', 'col'), may hold values from -0.21875 to 0.21875
- factors: float32 [8, 256, 256], P('col'), may hold values from -3 to 3, as said below
Outputs:
- transformed: float32 [98304, 2048], P('row', 'col')
Inputs may be any that keep to these rules, and one draw needn't show every extreme that they name: Each slab of factors is upper triangular with its diagonal between 0.5 and 2.
All inputs are finite; a program needn't handle non-finite values.
Results may differ from a plain program's by a relative error of at most 0.00017.
Values sent between devices are 32-bit elements; how exact they have to be, the bound alone decides.
A program may use at most 64 MiB of HBM per device.

v0:
```python
import jax
import jax.numpy as jnp
from jax import lax
from jax.sharding import PartitionSpec as P


def from_root(value, axis, source):
    kept = jnp.where(lax.axis_index(axis) == source, value, 0).astype(value.dtype)
    return lax.psum(kept, axis)


def matmul(left, right):
    return jnp.dot(left, right, precision=lax.Precision.HIGHEST, preferred_element_type=jnp.float32)


def project(vectors, field):
    return lax.dot_general(
        vectors,
        field,
        (((0,), (0,)), ((), ())),
        precision=lax.Precision.HIGHEST,
        preferred_element_type=jnp.float32,
    )


def scaled_sum(partial_terms, factor):
    summed = lax.psum(partial_terms, "row")
    return matmul(factor, summed)


def local(eigvecs, reflectors, factors):
    first_v, first_t = (from_root(reflectors, "col", 1), from_root(factors, "col", 1))
    second_v, second_t = (from_root(reflectors, "col", 0), from_root(factors, "col", 0))
    first_t = first_t[0]
    second_t = second_t[0]
    scaled_first = scaled_sum(project(first_v, eigvecs), first_t)
    middle = eigvecs - matmul(first_v, scaled_first)
    scaled_second = scaled_sum(project(second_v, middle), second_t)
    return middle - matmul(second_v, scaled_second)


def solution(mesh):
    in_specs = (P("row", "col"), P("row", "col"), P("col", None, None))
    out_specs = P("row", "col")
    return jax.shard_map(local, mesh=mesh, in_specs=in_specs, out_specs=out_specs, check_vma=False)
```

profile of v0, /device:TPU:9, one launch (start us, length us, event | category | flops | bytes accessed | tf_op | source)
XLA Modules:
  0.0 426.6 jit_solution(6520332960287249788)
XLA Ops:
  6.5 0.0 all-reduce.9.cloned.1.call-start
  6.5 1.8 select_bitcast_fusion
  8.3 5.0 %broadcast_select_fusion = (f32[3072,256]{1,0:T(8,128)}, f32[3072,256]{1,0:T(8,128)}) fusion(f32[3072,256]{1,0:T(8,128)} %param.4, pred[]{:T(512)S(6)} %eq.9, pred[]{:T(512)S(6)} %eq.8), kind=kLoop, calls=%fused_computation.2 | loop fusion | flops 1572864 | bytes 9437186 | tf_op jit(solution)/shard_map/jit(_where)/select_n | solution.py:8
  13.4 0.0 copy-start
  13.4 0.0 all-reduce.9.cloned.1.call-update
  13.4 0.0 all-reduce.5.cloned.1.call-start
  13.4 97.0 %all-reduce.9.cloned.1.call-done = (f32[3072,256]{1,0:T(8,128)}, f32[256,256]{1,0:T(8,128)}, f32[3072,256]{1,0:T(8,128)}, f32[256,256]{1,0:T(8,128)}) async-done(((f32[3072,256]{1,0:T(8,128)}, f32[256,256]{1,0:T(8,128)}, f32[3072,256]{1,0:T(8,128)}, f32[256,256]{1,0:T(8,128)}), (f32[3072,256]{1,0:T(8,128)}, f32[256,256]{1,0:T(8,128)}, f32[3072,256]{1,0:T(8,128)}, ...) | async-done | bytes 6815760 | tf_op jit(solution)/shard_map/psum | solution.py:9
  110.5 0.0 copy-done
  110.5 0.0 copy-start.3
  110.5 7.7 %fusion = f32[256,256]{1,0:T(8,128)} fusion(f32[3072,256]{1,0:T(8,128)} %get-tuple-element.5, f32[3072,256]{1,0:T(8,128)S(1)} %copy-done), kind=kOutput, calls=%fused_computation.6 | convolution fusion | flops 2415919104 | bytes 6553600 | tf_op jit(solution)/shard_map/dot_general | solution.py:17
  118.2 0.0 all-reduce.5.cloned.1.call-update
  118.2 0.2 all-reduce.7.cloned.1.call-start
  118.5 140.0 %all-reduce.5.cloned.1.call-done = f32[256,256]{1,0:T(8,128)} async-done(((f32[256,256]{1,0:T(8,128)}), f32[256,256]{1,0:T(8,128)}) %all-reduce.5.cloned.1.call-update) | async-done | bytes 262160 | tf_op jit(solution)/shard_map/psum | solution.py:27
  258.4 0.0 copy-done.3
  258.4 1.3 fusion.1
  259.8 0.0 copy-start.1
  259.8 5.6 %convolution_subtract_fusion.1 = f32[3072,256]{1,0:T(8,128)S(1)} fusion(f32[3072,256]{1,0:T(8,128)} %param.3, f32[3072,256]{1,0:T(8,128)} %get-tuple-element.5, f32[256,256]{1,0:T(8,128)S(1)} %fusion.1), kind=kOutput, calls=%fused_computation.1 | convolution fusion | flops 2416705536 | bytes 9699328 | tf_op jit(solution)/shard_map/dot_general | solution.py:13
  265.4 0.0 copy-done.1
  265.4 0.0 copy-start.2
  265.4 6.0 %fusion.2 = f32[256,256]{1,0:T(8,128)} fusion(f32[3072,256]{1,0:T(8,128)S(1)} %copy-done.1, f32[3072,256]{1,0:T(8,128)S(1)} %convolution_subtract_fusion.1), kind=kOutput, calls=%fused_computation.8 | convolution fusion | flops 2415919104 | bytes 6553600 | tf_op jit(solution)/shard_map/dot_general | solution.py:17
  271.4 0.0 all-reduce.7.cloned.1.call-update
  271.4 141.2 %all-reduce.7.cloned.1.call-done = f32[256,256]{1,0:T(8,128)} async-done(((f32[256,256]{1,0:T(8,128)}), f32[256,256]{1,0:T(8,128)}) %all-reduce.7.cloned.1.call-update) | async-done | bytes 262160 | tf_op jit(solution)/shard_map/psum | solution.py:27
  412.6 0.0 copy-done.2
  412.6 1.3 fusion.3
  413.9 6.2 %convolution_subtract_fusion = f32[3072,256]{1,0:T(8,128)} fusion(f32[3072,256]{1,0:T(8,128)S(1)} %convolution_subtract_fusion.1, f32[3072,256]{1,0:T(8,128)} %get-tuple-element.7, f32[256,256]{1,0:T(8,128)S(1)} %fusion.3), kind=kOutput, calls=%fused_computation | convolution fusion | flops 2416705536 | bytes 9699328 | tf_op jit(solution)/shard_map/dot_general | solution.py:13
Async XLA Ops:
  6.5 103.9 %all-reduce.9.cloned.1.call-start = ((), (), s32[]{:S(2)}) async-start(), calls=%async_computation.2 | async-start | bytes 13631488 | tf_op jit(solution)/shard_map/psum | solution.py:9
  13.4 97.1 %copy-start = (f32[3072,256]{1,0:T(8,128)S(1)}, f32[3072,256]{1,0:T(8,128)}, u32[]{:S(2)}) copy-start(f32[3072,256]{1,0:T(8,128)} %param.3) | copy-start | bytes 9437188
  13.4 245.0 %all-reduce.5.cloned.1.call-start = ((), (), s32[]{:S(2)}) async-start(), calls=%async_computation | async-start | bytes 524288 | tf_op jit(solution)/shard_map/psum | solution.py:27
  110.5 148.0 %copy-start.3 = (f32[256,256]{1,0:T(8,128)S(1)}, f32[256,256]{1,0:T(8,128)}, u32[]{:S(2)}) copy-start(f32[256,256]{1,0:T(8,128)} %get-tuple-element.6) | copy-start | bytes 786436
  118.2 294.4 %all-reduce.7.cloned.1.call-start = ((), (), s32[]{:S(2)}) async-start(), calls=%async_computation.1 | async-start | bytes 524288 | tf_op jit(solution)/shard_map/psum | solution.py:27
  259.8 5.6 %copy-start.1 = (f32[3072,256]{1,0:T(8,128)S(1)}, f32[3072,256]{1,0:T(8,128)}, u32[]{:S(2)}) copy-start(f32[3072,256]{1,0:T(8,128)} %get-tuple-element.7) | copy-start | bytes 9437188
  265.4 147.2 %copy-start.2 = (f32[256,256]{1,0:T(8,128)S(1)}, f32[256,256]{1,0:T(8,128)}, u32[]{:S(2)}) copy-start(f32[256,256]{1,0:T(8,128)} %get-tuple-element.8) | copy-start | bytes 786436
Sparse Core Ops, SparseCore 0:
  13.5 96.9 all-reduce.8
  118.4 140.0 all-reduce.4
  271.5 140.9 all-reduce.6
where the time goes:
time: 431 us; the launch traced here: 427 us
  waiting for transfers between devices  378 us (88%)
  matrix products  28.2 us (7%)
  between operations  13.2 us (3%)
  other arithmetic  6.82 us (2%)
    psum x2, waiting for transfers between devices, scaled_sum(): summed = lax.psum(partial_terms, 'row')  281 us
    psum x1, waiting for transfers between devices, from_root(): return lax.psum(kept, axis)  97 us
    dot_general x4, matrix products, matmul(): jnp.dot(left, right, precision=lax.Precision.HIGHEST, preferred_element_t...  14.4 us
    dot_general x2, matrix products, project(): lax.dot_general(vectors, field, (((0,), (0,)), ((), ())), precision=lax.P...  13.7 us
  transfers between devices with their start and end apart: 3, of which 3 were waited for; matrix products, arithmetic and copies ran while one was open for 0% of the time, Pallas kernels for 0%

commit v1 on v0

v1 whole, which is shorter than its diff:
```python
import jax
import jax.numpy as jnp
from jax import lax
from jax.experimental import pallas as pl
from jax.experimental.pallas import tpu as pltpu
from jax.sharding import PartitionSpec as P

MESH = pl.DeviceIdType.MESH
F32, BF16 = jnp.float32, jnp.bfloat16
NZ, NX, NCOL = 8, 4, 8
NB = 256
ROWS = 3072
HALF = ROWS // 2
TICK = 16
GROUP = 64
TICKS = GROUP // TICK
PER_PANEL = NB // GROUP
GROUPS = 2 * PER_PANEL
CHUNKS = GROUPS * TICKS
TILE = 128


def split(value):
    high = value.astype(BF16)
    return high, (value - high.astype(F32)).astype(BF16)


def dot(left, right):
    return jnp.dot(left, right, preferred_element_type=F32)


def dot_nt(left, right):
    return lax.dot_general(left, right, (((1,), (1,)), ((), ())), preferred_element_type=F32)


def product(left, right):
    lh, ll = split(left)
    rh, rl = split(right)
    return dot(lh, rh) + dot(lh, rl) + dot(ll, rh)


def kernel(
    e_hbm, v_hbm, f_hbm, out_hbm,
    e, raw, eh, el, vt, vn,
    wloc, rs_land, xs, x_land, red, ag_land, wfull,
    ms, mz_land, mz, mx_land, mats,
    gacc, gloc, gz_land, gq, gx_land,
    s_stack, s_low,
    load_sem, out_sem, recv, send, sib,
    rs_s, rs_r, x_s, x_r, ag_s, ag_r,
    ms_s, ms_r, mz_s, mz_r, mx_s, mx_r,
    gz_s, gz_r, gx_s, gx_r,
):
    row = lax.axis_index("row")
    col = lax.axis_index("col")
    z, x = row // NX, row % NX
    y, core = col // 2, col % 2

    def ring(yy, cc):
        return (row, yy * 2 + cc)

    def z_peer(d):
        return (lax.rem(z + d, NZ) * NX + x, col)

    def x_peer(d):
        return (z * NX + lax.rem(x + d, NX), col)

    at_root = y == 0
    first = ((core == 1) & (y == 1)) | ((core == 0) & (y == 3))
    last = ((core == 1) & (y == 3)) | ((core == 0) & (y == 1))
    ahead = jnp.where(core == 1, y + 1, y - 1)
    behind = jnp.where(core == 1, y - 1, y + 1)
    lag = jnp.where(first, 2, 1)
    mine = 1 - core
    rank = x * NZ + z

    def remote(src, dst, send_sem, recv_sem, device):
        return pltpu.make_async_remote_copy(
            src_ref=src, dst_ref=dst, send_sem=send_sem, recv_sem=recv_sem, device_id=device, device_id_type=MESH
        )

    load_e = pltpu.make_async_copy(e_hbm, e, load_sem.at[0])
    load_v = pltpu.make_async_copy(v_hbm, raw, load_sem.at[1])
    load_f = pltpu.make_async_copy(
        f_hbm.at[0, pl.ds(pl.multiple_of(rank * 8, 8), 8), :], ms.at[1 - core], load_sem.at[2]
    )

    @pl.when(at_root)
    def _():
        load_v.start()
        load_f.start()

    load_e.start()

    barrier = pltpu.get_barrier_semaphore()

    def greet(device):
        pl.semaphore_signal(barrier, inc=1, device_id=device, device_id_type=MESH)

    for d in range(1, NZ):
        greet(z_peer(d))
    for d in range(1, NX):
        greet(x_peer(d))
    greet(ring(y, 1 - core))

    @pl.when(jnp.logical_not(at_root))
    def _():
        greet(ring(0, 0))
        greet(ring(0, 1))

    @pl.when(jnp.logical_not(at_root | first))
    def _():
        greet(ring(behind, core))

    def transpose_in(ct):
        panel = 1 - core

        def body(rt, _):
            start = pl.multiple_of(rt * TILE, TILE)
            for h in range(2):
                block = raw[pl.ds(pl.multiple_of(h * HALF + start, TILE), TILE), ct * TILE : (ct + 1) * TILE]
                vt[panel, h, ct * TILE : (ct + 1) * TILE, pl.ds(start, TILE)] = block.T
            return 0

        lax.fori_loop(0, HALF // TILE, body, 0)

    @pl.when(at_root)
    def _():
        load_v.wait()
        load_f.wait()
        transpose_in(0)

    pl.semaphore_wait(barrier, (NZ - 1) + (NX - 1) + jnp.where(at_root, 7, jnp.where(last, 1, 2)))

    def spread(m):
        for d in range(1, NCOL):
            yield remote(ms.at[m], ms.at[m], ms_s.at[m], ms_r.at[m], (row, lax.rem(col + d, NCOL)))

    for m in range(2):

        @pl.when(at_root & (core == 1 - m))
        def _():
            for copy in spread(m):
                copy.start()

    def row0(g):
        return pl.multiple_of(jnp.where(g < PER_PANEL, g, GROUPS - 1 - g) * GROUP, GROUP)

    def chunk(k, h):
        g = k // TICKS
        start = pl.multiple_of(row0(g) + (k % TICKS) * TICK, TICK)
        return vt.at[g // PER_PANEL, h, pl.ds(start, TICK), :]

    def piece(k, h, send_sem, device):
        ref = chunk(k, h)
        return remote(ref, ref, send_sem, recv.at[h, k], device)

    def ring_send(k, h):
        return piece(k, h, send.at[h, k], ring(jnp.where(h == 0, 1, 3), jnp.where(h == 0, 1, 0)))

    def sib_send(k, h):
        return piece(k, h, sib.at[h, k], ring(y, 1 - core))

    def ahead_send(k):
        return piece(k, mine, send.at[0, k], ring(ahead, core))

    def pass_on(k):
        return piece(k, mine, sib.at[0, k], ring(y, 1 - core))

    def arrived(k, h):
        piece(k, h, send.at[0, k], ring(y, 1 - core)).wait_recv()

    def ticks(i, begin, end):
        owner = at_root & ((core == 1) == (i < PER_PANEL))
        follower = at_root & ((core == 0) == (i < PER_PANEL))

        for t in range(begin, end):
            k = i * TICKS + t

            @pl.when(owner)
            def _():
                @pl.when(i % PER_PANEL != 0)
                def _():
                    for h in range(2):
                        ring_send(k - TICKS, h).wait_send()

                for h in range(2):
                    ring_send(k, h).start()
                for h in range(2):
                    sib_send(k, h).start()

            @pl.when(follower)
            def _():
                arrived(k, 0)
                arrived(k, 1)

            @pl.when(jnp.logical_not(at_root))
            def _():
                arrived(k, mine)

                @pl.when(jnp.logical_not(last))
                def _():
                    ahead_send(k).start()

                pass_on(k).start()

    def to_z(g):
        for d in range(1, NZ):
            to = lax.rem(z + d, NZ)
            yield remote(
                wloc.at[g, pl.ds(pl.multiple_of(to * 8, 8), 8), :],
                rs_land.at[g, d - 1], rs_s.at[g], rs_r.at[g], z_peer(d),
            )

    def to_x(g):
        for d in range(1, NX):
            yield remote(xs.at[g], x_land.at[g, d - 1], x_s.at[g], x_r.at[g], x_peer(d))

    def back_z(g):
        for d in range(1, NZ):
            yield remote(red.at[g], ag_land.at[g, d - 1], ag_s.at[g], ag_r.at[g], z_peer(d))

    def whole(ref, send_sem, recv_sem):
        return remote(ref, ref, send_sem, recv_sem, ring(y, 1 - core))

    def project(g):
        total = jnp.zeros((GROUP, NB), F32)
        for h in range(2):
            high, low = split(vt[g // PER_PANEL, h, pl.ds(row0(g), GROUP), :])
            both = dot(jnp.concatenate([high, low], axis=0), eh[h * HALF : (h + 1) * HALF, :])
            total += both[:GROUP] + both[GROUP:] + dot(high, el[h * HALF : (h + 1) * HALF, :])
        wloc[g] = total
        for copy in to_z(g):
            copy.start()

    def sum_z(g):
        whole(rs_land.at[g], rs_s.at[g], rs_r.at[g]).wait_recv()
        total = wloc[g, pl.ds(pl.multiple_of(z * 8, 8), 8), :]
        for d in range(NZ - 1):
            total += rs_land[g, d]
        xs[g] = total
        for copy in to_x(g):
            copy.start()

    def sum_x(g):
        whole(x_land.at[g], x_s.at[g], x_r.at[g]).wait_recv()
        total = xs[g]
        for d in range(NX - 1):
            total += x_land[g, d]
        red[g] = total
        for copy in back_z(g):
            copy.start()

    def gather(g):
        whole(ag_land.at[g], ag_s.at[g], ag_r.at[g]).wait_recv()
        base = (g // PER_PANEL) * NB + row0(jnp.int32(g))
        wfull[pl.ds(pl.multiple_of(base + z * 8, 8), 8), :] = red[g]
        for d in range(1, NZ):
            origin = lax.rem(z + NZ - d, NZ)
            wfull[pl.ds(pl.multiple_of(base + origin * 8, 8), 8), :] = ag_land[g, d - 1]

    def tile_column(j):
        return pl.multiple_of(jnp.where((j == 1) | (j == 2), TILE, 0), TILE)

    def transpose_out(j, h):
        def body(rt, _):
            start = pl.multiple_of(rt * TILE, TILE)
            block = vt[j // 2, h, pl.ds(tile_column(j), TILE), pl.ds(start, TILE)]
            high, low = split(block.T)
            rows = pl.ds(pl.multiple_of(h * HALF + start, TILE), TILE)
            vn[j, rows, :TILE] = high
            vn[j, rows, TILE:] = low
            return 0

        lax.fori_loop(0, HALF // TILE, body, 0)

    def m_to_z(m):
        for d in range(1, NZ):
            yield remote(ms.at[m], mz_land.at[m, d - 1], mz_s.at[m], mz_r.at[m], z_peer(d))

    def m_to_x(m):
        for d in range(1, NX):
            yield remote(mz.at[m], mx_land.at[m, d - 1], mx_s.at[m], mx_r.at[m], x_peer(d))

    def m_begin(m):
        is_source = at_root & ((core == 1) if m == 0 else (core == 0))

        @pl.when(jnp.logical_not(is_source))
        def _():
            whole(ms.at[m], ms_s.at[m], ms_r.at[m]).wait_recv()

        for copy in m_to_z(m):
            copy.start()

    def m_middle(m):
        whole(mz_land.at[m], mz_s.at[m], mz_r.at[m]).wait_recv()
        mz[m, pl.ds(pl.multiple_of(z * 8, 8), 8), :] = ms[m]
        for d in range(1, NZ):
            origin = lax.rem(z + NZ - d, NZ)
            mz[m, pl.ds(pl.multiple_of(origin * 8, 8), 8), :] = mz_land[m, d - 1]
        for copy in m_to_x(m):
            copy.start()

    def m_end(m):
        whole(mx_land.at[m], mx_s.at[m], mx_r.at[m]).wait_recv()
        mats[m, pl.ds(pl.multiple_of(x * 64, 64), 64), :] = mz[m]
        for d in range(1, NX):
            origin = lax.rem(x + NX - d, NX)
            mats[m, pl.ds(pl.multiple_of(origin * 64, 64), 64), :] = mx_land[m, d - 1]

    overlap_here = at_root & (core == 0)

    def overlap_to_z():
        for d in range(1, NZ):
            yield remote(gloc.at[lax.rem(z + d, NZ)], gz_land.at[d - 1], gz_s.at[0], gz_r.at[0], z_peer(d))

    def overlap_to_x():
        for d in range(1, NX):
            yield remote(gq.at[lax.rem(x + d, NX)], gx_land.at[d - 1], gx_s.at[0], gx_r.at[0], x_peer(d))

    def overlap_begin():
        gacc[...] = jnp.zeros_like(gacc)

        def body(n, _):
            h, part = n // 3, n % 3
            lanes = pl.ds(pl.multiple_of(part * 512, 512), 512)
            ah, al = split(vt[1, h, :, lanes])
            bh, bl = split(vt[0, h, :, lanes])
            gacc[...] += dot_nt(ah, bh) + dot_nt(ah, bl) + dot_nt(al, bh)
            return 0

        lax.fori_loop(0, 6, body, 0)
        for zz in range(NZ):
            for xx in range(NX):
                gloc[zz, xx] = gacc[xx * 64 + zz * 8 : xx * 64 + zz * 8 + 8, :]
        for copy in overlap_to_z():
            copy.start()

    def overlap_middle():
        whole(gz_land, gz_s.at[0], gz_r.at[0]).wait_recv()
        total = gloc[z]
        for d in range(NZ - 1):
            total += gz_land[d]
        gq[...] = total
        for copy in overlap_to_x():
            copy.start()

    def overlap_end():
        whole(gx_land, gx_s.at[0], gx_r.at[0]).wait_recv()
        total = gq[x]
        for d in range(NX - 1):
            total += gx_land[d]
        ms[2] = total
        for copy in spread(2):
            copy.start()

    def split_field():
        load_e.wait()

        def body(n, _):
            rows = pl.ds(pl.multiple_of(n * 256, 256), 256)
            high, low = split(e[rows, :])
            eh[rows, :] = high
            el[rows, :] = low
            return 0

        lax.fori_loop(0, ROWS // 256, body, 0)

    def when(condition, action, *args):
        pl.when(condition)(lambda: action(*args))

    def step(i, _):
        done = i - lag
        when(i < GROUPS, ticks, i, 0, 2)

        @pl.when(i == 0)
        def _():
            split_field()
            when(at_root, transpose_in, 1)

        when(done >= 0, project, done)
        when(i < GROUPS, ticks, i, 2, TICKS)
        when(done >= 1, lambda: transpose_out((done - 1) // 2, (done - 1) % 2))
        when(done >= 2, sum_z, done - 2)
        when(done >= 4, sum_x, done - 4)

        @pl.when(done == 1)
        def _():
            m_begin(0)
            m_begin(1)

        @pl.when(done == 3)
        def _():
            m_middle(0)
            m_middle(1)

        when(overlap_here & (i == 4), overlap_begin)
        when(overlap_here & (i == 6), overlap_middle)
        when(overlap_here & (i == 7), overlap_end)
        return 0

    def step_with_sibling(i, carry):
        done = i - lag

        @pl.when((done >= 0) & jnp.logical_not(at_root))
        def _():
            for t in range(TICKS):
                arrived(done * TICKS + t, core)

        return step(i, carry)

    lax.fori_loop(0, GROUPS + lag, step_with_sibling, 0)

    def set_s(j, value):
        high, low = split(value)
        s_stack[j, :TILE] = high
        s_stack[j, TILE:] = high
        s_low[j] = low

    def update(tiles, finish):
        def body(n, _):
            rows = pl.ds(pl.multiple_of(n * 512, 512), 512)
            total = e[rows, :]
            for j in tiles:
                part = vn[j, rows, :]
                total -= dot(part, s_stack[j]) + dot(part[:, :TILE], s_low[j])
            e[rows, :] = total
            if finish:
                pltpu.make_async_copy(e.at[rows], out_hbm.at[rows], out_sem.at[n]).start()
            return 0

        lax.fori_loop(0, ROWS // 512, body, 0)

    m_begin(2)
    sum_z(6)
    sum_x(4)
    m_end(0)
    m_end(1)
    transpose_out(3, 1)
    sum_z(7)
    sum_x(5)
    sum_x(6)
    m_middle(2)
    for g in range(4):
        gather(g)
    first_s = product(mats[0], wfull[:NB, :])
    set_s(0, first_s[:TILE])
    set_s(1, first_s[TILE:])
    sum_x(7)
    update((0, 1), False)
    m_end(2)
    gather(4)
    gather(5)
    correction = product(mats[2], first_s)
    upper = wfull[NB + TILE :, :] - correction[TILE:]
    set_s(2, product(mats[1, TILE:, TILE:], upper))
    update((2,), False)
    gather(6)
    gather(7)
    lower = wfull[NB : NB + TILE, :] - correction[:TILE]
    set_s(3, product(mats[1, :TILE, :], jnp.concatenate([lower, upper], axis=0)))
    update((3,), True)

    for g in range(GROUPS):
        whole(rs_land.at[g], rs_s.at[g], rs_r.at[g]).wait_send()
        whole(x_land.at[g], x_s.at[g], x_r.at[g]).wait_send()
        whole(ag_land.at[g], ag_s.at[g], ag_r.at[g]).wait_send()
    for m in range(3):
        whole(mz_land.at[m], mz_s.at[m], mz_r.at[m]).wait_send()
        whole(mx_land.at[m], mx_s.at[m], mx_r.at[m]).wait_send()

        @pl.when(at_root & ((core == 1) if m == 0 else (core == 0)))
        def _():
            whole(mz_land.at[m], ms_s.at[m], ms_r.at[m]).wait_send()

    @pl.when(overlap_here)
    def _():
        whole(gz_land, gz_s.at[0], gz_r.at[0]).wait_send()
        whole(gx_land, gx_s.at[0], gx_r.at[0]).wait_send()

    def drain(k, _):
        @pl.when(jnp.logical_not(at_root))
        def _():
            @pl.when(jnp.logical_not(last))
            def _():
                ahead_send(k).wait_send()

            pass_on(k).wait_send()

        @pl.when(at_root & ((core == 1) == (k < CHUNKS // 2)))
        def _():
            for h in range(2):
                sib_send(k, h).wait_send()

                @pl.when(k % (CHUNKS // 2) >= CHUNKS // 2 - TICKS)
                def _():
                    ring_send(k, h).wait_send()

        return 0

    lax.fori_loop(0, CHUNKS, drain, 0)

    def finish(n, _):
        rows = pl.ds(pl.multiple_of(n * 512, 512), 512)
        pltpu.make_async_copy(e.at[rows], out_hbm.at[rows], out_sem.at[n]).wait()
        return 0

    lax.fori_loop(0, ROWS // 512, finish, 0)


def local(eigvecs, reflectors, factors):
    vmem, dma = pltpu.VMEM, pltpu.SemaphoreType.DMA
    anywhere = pl.BlockSpec(memory_space=pl.ANY)
    return pl.pallas_call(
        kernel,
        out_shape=jax.ShapeDtypeStruct((ROWS, NB), F32),
        in_specs=[anywhere] * 3,
        out_specs=anywhere,
        scratch_shapes=[
            vmem((ROWS, NB), F32),
            vmem((ROWS, NB), F32),
            vmem((ROWS, NB), BF16),
            vmem((ROWS, NB), BF16),
            vmem((2, 2, NB, HALF), F32),
            vmem((4, ROWS, NB), BF16),
            vmem((GROUPS, GROUP, NB), F32),
            vmem((GROUPS, NZ - 1, 8, NB), F32),
            vmem((GROUPS, 8, NB), F32),
            vmem((GROUPS, NX - 1, 8, NB), F32),
            vmem((GROUPS, 8, NB), F32),
            vmem((GROUPS, NZ - 1, 8, NB), F32),
            vmem((2 * NB, NB), F32),
            vmem((3, 8, NB), F32),
            vmem((3, NZ - 1, 8, NB), F32),
            vmem((3, 64, NB), F32),
            vmem((3, NX - 1, 64, NB), F32),
            vmem((3, NB, NB), F32),
            vmem((NB, NB), F32),
            vmem((NZ, NX, 8, NB), F32),
            vmem((NZ - 1, NX, 8, NB), F32),
            vmem((NX, 8, NB), F32),
            vmem((NX - 1, 8, NB), F32),
            vmem((4, NB, NB), BF16),
            vmem((4, TILE, NB), BF16),
            dma((3,)),
            dma((ROWS // 512,)),
            dma((2, CHUNKS)),
            dma((2, CHUNKS)),
            dma((2, CHUNKS)),
            *[dma((GROUPS,))] * 6,
            *[dma((3,))] * 6,
            *[dma((1,))] * 4,
        ],
        compiler_params=pltpu.CompilerParams(collective_id=0, has_side_effects=True, vmem_limit_bytes=50 * 2**20),
    )(eigvecs, reflectors, factors)


def solution(mesh):
    in_specs = (P("row", "col"), P("row", "col"), P("col", None, None))
    return jax.shard_map(local, mesh=mesh, in_specs=in_specs, out_specs=P("row", "col"), check_vma=False)
```

time: 431 us -> 85.4 us (0.20)
  the two profiles are of different devices: /device:TPU:9 before, /device:TPU:8 now
where the time goes in v1:
time: 85.4 us; the launch traced here: 85.3 us
  Pallas kernels  82.7 us (97%)
  local copies, waits for them, and re-layouts  2.62 us (3%)
    pallas_call x1, Pallas kernels, local(): pl.pallas_call(kernel, out_shape=jax.ShapeDtypeStruct((ROWS, NB), F32), i...  82.7 us
    unnamed x3, local copies, waits for them, and re-layouts  2.62 us

profile of v1, /device:TPU:8, one launch (start us, length us, event | category | flops | bytes accessed | tf_op | source)
XLA Modules:
  0.0 85.3 jit_solution(8964412073547564326)
XLA Ops:
  0.0 0.0 copy-start
  0.0 0.9 %copy-done = f32[1,256,256]{2,1,0:T(8,128)S(1)} copy-done((f32[1,256,256]{2,1,0:T(8,128)S(1)}, f32[1,256,256]{2,1,0:T(8,128)}, u32[]{:S(2)}) %copy-start) | copy-done | bytes 262168
  1.0 82.7 %shard_map.37 = f32[3072,256]{1,0:T(8,128)S(1)} custom-call(f32[3072,256]{1,0:T(8,128)} %e_hbm.1, f32[3072,256]{1,0:T(8,128)} %v_hbm.1, f32[1,256,256]{2,1,0:T(8,128)S(1)} %copy-done), custom_call_target="tpu_custom_call" | custom-call | tf_op jit(solution)/shard_map/pallas_call | solution.py:514
  83.6 1.7 %copy.5 = f32[3072,256]{1,0:T(8,128)} copy(f32[3072,256]{1,0:T(8,128)S(1)} %shard_map.37) | data formatting | bytes 6291456
Async XLA Ops:
  0.0 0.9 %copy-start = (f32[1,256,256]{2,1,0:T(8,128)S(1)}, f32[1,256,256]{2,1,0:T(8,128)}, u32[]{:S(2)}) copy-start(f32[1,256,256]{2,1,0:T(8,128)} %f_hbm.1) | copy-start | bytes 786436

commit v2 on v1

--- a/solution.py
+++ b/solution.py
@@ -18,6 +18,9 @@
 GROUPS = 2 * PER_PANEL
 CHUNKS = GROUPS * TICKS
 TILE = 128
+DEPTH = 3
+DIRECT = CHUNKS - 2
+UNITS = GROUPS + 1
 
 
 def split(value):
@@ -42,12 +45,12 @@
 def kernel(
     e_hbm, v_hbm, f_hbm, out_hbm,
     e, raw, eh, el, vt, vn,
-    wloc, rs_land, xs, x_land, red, ag_land, wfull,
+    wloc, x_land, zs, z_land, red, ag_land, wfull,
     ms, mz_land, mz, mx_land, mats,
     gacc, gloc, gz_land, gq, gx_land,
     s_stack, s_low,
     load_sem, out_sem, recv, send, sib,
-    rs_s, rs_r, x_s, x_r, ag_s, ag_r,
+    direct, x_s, x_r, z_s, z_r, ag_s, ag_r,
     ms_s, ms_r, mz_s, mz_r, mx_s, mx_r,
     gz_s, gz_r, gx_s, gx_r,
 ):
@@ -70,7 +73,7 @@
     last = ((core == 1) & (y == 3)) | ((core == 0) & (y == 1))
     ahead = jnp.where(core == 1, y + 1, y - 1)
     behind = jnp.where(core == 1, y - 1, y + 1)
-    lag = jnp.where(first, 2, 1)
+    lag = jnp.where(first, 4, jnp.where(y == 2, 2, 1))
     mine = 1 - core
     rank = x * NZ + z
 
@@ -158,6 +161,12 @@
     def ring_send(k, h):
         return piece(k, h, send.at[h, k], ring(jnp.where(h == 0, 1, 3), jnp.where(h == 0, 1, 0)))
 
+    def direct_send(k, h):
+        return piece(k, h, direct.at[h, k - DIRECT], ring(jnp.where(h == 0, 3, 1), jnp.where(h == 0, 1, 0)))
+
+    def relays(k):
+        return jnp.logical_not(last | ((y == 2) & (k >= DIRECT)))
+
     def sib_send(k, h):
         return piece(k, h, sib.at[h, k], ring(y, 1 - core))
 
@@ -179,13 +188,19 @@
 
             @pl.when(owner)
             def _():
-                @pl.when(i % PER_PANEL != 0)
+                @pl.when(k % (CHUNKS // 2) >= DEPTH)
                 def _():
                     for h in range(2):
-                        ring_send(k - TICKS, h).wait_send()
+                        ring_send(k - DEPTH, h).wait_send()
 
                 for h in range(2):
                     ring_send(k, h).start()
+
+                @pl.when(k >= DIRECT)
+                def _():
+                    for h in range(2):
+                        direct_send(k, h).start()
+
                 for h in range(2):
                     sib_send(k, h).start()
 
@@ -198,66 +213,88 @@
             def _():
                 arrived(k, mine)
 
-                @pl.when(jnp.logical_not(last))
+                @pl.when(relays(k))
                 def _():
                     ahead_send(k).start()
 
                 pass_on(k).start()
 
-    def to_z(g):
+    def share(u):
+        return 8 if isinstance(u, int) and u >= GROUPS - 1 else 16
+
+    def first_column(u):
+        if isinstance(u, int) and u == GROUPS:
+            return 32
+        return row0(jnp.int32(u) if isinstance(u, int) else u)
+
+    def panel_of(u):
+        return 1 if isinstance(u, int) and u >= PER_PANEL else u // PER_PANEL
+
+    def part(ref, u):
+        return ref.at[u] if share(u) == 16 else ref.at[u, :, pl.ds(0, 8), :]
+
+    def own(u, position):
+        return pl.ds(pl.multiple_of(position * share(u), 8), share(u))
+
+    def to_x(u):
+        for d in range(1, NX):
+            yield remote(
+                wloc.at[u, own(u, lax.rem(x + d, NX)), :],
+                x_land.at[u, d - 1, pl.ds(0, share(u)), :], x_s.at[u], x_r.at[u], x_peer(d),
+            )
+
+    def to_z(u):
         for d in range(1, NZ):
-            to = lax.rem(z + d, NZ)
-            yield remote(
-                wloc.at[g, pl.ds(pl.multiple_of(to * 8, 8), 8), :],
-                rs_land.at[g, d - 1], rs_s.at[g], rs_r.at[g], z_peer(d),
-            )
-
-    def to_x(g):
+            ref = zs.at[u, pl.ds(0, share(u)), :]
+            yield remote(ref, z_land.at[u, d - 1, pl.ds(0, share(u)), :], z_s.at[u], z_r.at[u], z_peer(d))
+
+    def back_x(u):
         for d in range(1, NX):
-            yield remote(xs.at[g], x_land.at[g, d - 1], x_s.at[g], x_r.at[g], x_peer(d))
-
-    def back_z(g):
-        for d in range(1, NZ):
-            yield remote(red.at[g], ag_land.at[g, d - 1], ag_s.at[g], ag_r.at[g], z_peer(d))
+            ref = red.at[u, pl.ds(0, share(u)), :]
+            yield remote(ref, ag_land.at[u, d - 1, pl.ds(0, share(u)), :], ag_s.at[u], ag_r.at[u], x_peer(d))
 
     def whole(ref, send_sem, recv_sem):
         return remote(ref, ref, send_sem, recv_sem, ring(y, 1 - core))
 
-    def project(g):
-        total = jnp.zeros((GROUP, NB), F32)
+    def project(u):
+        count = share(u) * NX
+        total = jnp.zeros((count, NB), F32)
         for h in range(2):
-            high, low = split(vt[g // PER_PANEL, h, pl.ds(row0(g), GROUP), :])
+            high, low = split(vt[panel_of(u), h, pl.ds(first_column(u), count), :])
             both = dot(jnp.concatenate([high, low], axis=0), eh[h * HALF : (h + 1) * HALF, :])
-            total += both[:GROUP] + both[GROUP:] + dot(high, el[h * HALF : (h + 1) * HALF, :])
-        wloc[g] = total
-        for copy in to_z(g):
-            copy.start()
-
-    def sum_z(g):
-        whole(rs_land.at[g], rs_s.at[g], rs_r.at[g]).wait_recv()
-        total = wloc[g, pl.ds(pl.multiple_of(z * 8, 8), 8), :]
+            total += both[:count] + both[count:] + dot(high, el[h * HALF : (h + 1) * HALF, :])
+        wloc[u, :count] = total
+        for copy in to_x(u):
+            copy.start()
+
+    def sum_x(u):
+        n = share(u)
+        whole(part(x_land, u), x_s.at[u], x_r.at[u]).wait_recv()
+        total = wloc[u, own(u, x), :]
+        for d in range(NX - 1):
+            total += x_land[u, d, :n]
+        zs[u, :n] = total
+        for copy in to_z(u):
+            copy.start()
+
+    def sum_z(u):
+        n = share(u)
+        whole(part(z_land, u), z_s.at[u], z_r.at[u]).wait_recv()
+        total = zs[u, :n]
         for d in range(NZ - 1):
-            total += rs_land[g, d]
-        xs[g] = total
-        for copy in to_x(g):
-            copy.start()
-
-    def sum_x(g):
-        whole(x_land.at[g], x_s.at[g], x_r.at[g]).wait_recv()
-        total = xs[g]
-        for d in range(NX - 1):
-            total += x_land[g, d]
-        red[g] = total
-        for copy in back_z(g):
-            copy.start()
-
-    def gather(g):
-        whole(ag_land.at[g], ag_s.at[g], ag_r.at[g]).wait_recv()
-        base = (g // PER_PANEL) * NB + row0(jnp.int32(g))
-        wfull[pl.ds(pl.multiple_of(base + z * 8, 8), 8), :] = red[g]
-        for d in range(1, NZ):
-            origin = lax.rem(z + NZ - d, NZ)
-            wfull[pl.ds(pl.multiple_of(base + origin * 8, 8), 8), :] = ag_land[g, d - 1]
+            total += z_land[u, d, :n]
+        red[u, :n] = total
+        for copy in back_x(u):
+            copy.start()
+
+    def gather(u):
+        n = share(u)
+        whole(part(ag_land, u), ag_s.at[u], ag_r.at[u]).wait_recv()
+        base = panel_of(u) * NB + first_column(u)
+        wfull[pl.ds(pl.multiple_of(base + x * n, 8), n), :] = red[u, :n]
+        for d in range(1, NX):
+            origin = lax.rem(x + NX - d, NX)
+            wfull[pl.ds(pl.multiple_of(base + origin * n, 8), n), :] = ag_land[u, d - 1, :n]
 
     def tile_column(j):
         return pl.multiple_of(jnp.where((j == 1) | (j == 2), TILE, 0), TILE)
@@ -369,20 +406,38 @@
     def when(condition, action, *args):
         pl.when(condition)(lambda: action(*args))
 
+    def other_half(done, begin, end):
+        @pl.when(jnp.logical_not(at_root))
+        def _():
+            for t in range(begin, end):
+                arrived(done * TICKS + t, core)
+
     def step(i, _):
         done = i - lag
-        when(i < GROUPS, ticks, i, 0, 2)
+        when(i < GROUPS, ticks, i, 0, 1)
 
         @pl.when(i == 0)
         def _():
-            split_field()
             when(at_root, transpose_in, 1)
 
-        when(done >= 0, project, done)
-        when(i < GROUPS, ticks, i, 2, TICKS)
+        @pl.when(done >= 0)
+        def _():
+            other_half(done, 0, TICKS)
+            project(done)
+
+        when(i < GROUPS, ticks, i, 1, 2)
+        when(done >= 1, sum_x, done - 1)
+        when(done >= 3, sum_z, done - 3)
+        when(i < GROUPS, ticks, i, 2, 3)
+
+        @pl.when((i == GROUPS - 1) & last)
+        def _():
+            other_half(GROUPS - 1, 0, TICKS // 2)
+            project(GROUPS - 1)
+
+        when(i == 0, split_field)
         when(done >= 1, lambda: transpose_out((done - 1) // 2, (done - 1) % 2))
-        when(done >= 2, sum_z, done - 2)
-        when(done >= 4, sum_x, done - 4)
+        when(i < GROUPS, ticks, i, 3, 4)
 
         @pl.when(done == 1)
         def _():
@@ -397,19 +452,18 @@
         when(overlap_here & (i == 4), overlap_begin)
         when(overlap_here & (i == 6), overlap_middle)
         when(overlap_here & (i == 7), overlap_end)
+        when(done == 6, m_begin, 2)
         return 0
 
-    def step_with_sibling(i, carry):
-        done = i - lag
-
-        @pl.when((done >= 0) & jnp.logical_not(at_root))
-        def _():
-            for t in range(TICKS):
-                arrived(done * TICKS + t, core)
-
-        return step(i, carry)
-
-    lax.fori_loop(0, GROUPS + lag, step_with_sibling, 0)
+    lax.fori_loop(0, GROUPS - 1 + lag, step, 0)
+
+    @pl.when(jnp.logical_not(last))
+    def _():
+        other_half(GROUPS - 1, 0, TICKS // 2)
+        project(GROUPS - 1)
+
+    other_half(GROUPS - 1, TICKS // 2, TICKS)
+    project(GROUPS)
 
     def set_s(j, value):
         high, low = split(value)
@@ -431,40 +485,43 @@
 
         lax.fori_loop(0, ROWS // 512, body, 0)
 
-    m_begin(2)
-    sum_z(6)
-    sum_x(4)
+    sum_x(6)
+    sum_z(4)
+    transpose_out(3, 0)
+    sum_x(7)
+    sum_x(8)
+    sum_z(5)
     m_end(0)
     m_end(1)
     transpose_out(3, 1)
-    sum_z(7)
-    sum_x(5)
-    sum_x(6)
     m_middle(2)
-    for g in range(4):
-        gather(g)
+    for u in range(4):
+        gather(u)
     first_s = product(mats[0], wfull[:NB, :])
     set_s(0, first_s[:TILE])
     set_s(1, first_s[TILE:])
-    sum_x(7)
+    sum_z(6)
     update((0, 1), False)
-    m_end(2)
+    sum_z(7)
+    sum_z(8)
     gather(4)
     gather(5)
+    m_end(2)
     correction = product(mats[2], first_s)
     upper = wfull[NB + TILE :, :] - correction[TILE:]
     set_s(2, product(mats[1, TILE:, TILE:], upper))
     update((2,), False)
     gather(6)
     gather(7)
+    gather(8)
     lower = wfull[NB : NB + TILE, :] - correction[:TILE]
     set_s(3, product(mats[1, :TILE, :], jnp.concatenate([lower, upper], axis=0)))
     update((3,), True)
 
-    for g in range(GROUPS):
-        whole(rs_land.at[g], rs_s.at[g], rs_r.at[g]).wait_send()
-        whole(x_land.at[g], x_s.at[g], x_r.at[g]).wait_send()
-        whole(ag_land.at[g], ag_s.at[g], ag_r.at[g]).wait_send()
+    for u in range(UNITS):
+        whole(part(x_land, u), x_s.at[u], x_r.at[u]).wait_send()
+        whole(part(z_land, u), z_s.at[u], z_r.at[u]).wait_send()
+        whole(part(ag_land, u), ag_s.at[u], ag_r.at[u]).wait_send()
     for m in range(3):
         whole(mz_land.at[m], mz_s.at[m], mz_r.at[m]).wait_send()
         whole(mx_land.at[m], mx_s.at[m], mx_r.at[m]).wait_send()
@@ -481,7 +538,7 @@
     def drain(k, _):
         @pl.when(jnp.logical_not(at_root))
         def _():
-            @pl.when(jnp.logical_not(last))
+            @pl.when(relays(k))
             def _():
                 ahead_send(k).wait_send()
 
@@ -492,9 +549,13 @@
             for h in range(2):
                 sib_send(k, h).wait_send()
 
-                @pl.when(k % (CHUNKS // 2) >= CHUNKS // 2 - TICKS)
+                @pl.when(k % (CHUNKS // 2) >= CHUNKS // 2 - DEPTH)
                 def _():
                     ring_send(k, h).wait_send()
+
+                @pl.when(k >= DIRECT)
+                def _():
+                    direct_send(k, h).wait_send()
 
         return 0
 
@@ -514,7 +575,7 @@
     return pl.pallas_call(
         kernel,
         out_shape=jax.ShapeDtypeStruct((ROWS, NB), F32),
-        in_specs=[anywhere] * 3,
+        in_specs=[pl.BlockSpec(memory_space=pltpu.HBM)] * 3,
         out_specs=anywhere,
         scratch_shapes=[
             vmem((ROWS, NB), F32),
@@ -523,12 +584,12 @@
             vmem((ROWS, NB), BF16),
             vmem((2, 2, NB, HALF), F32),
             vmem((4, ROWS, NB), BF16),
-            vmem((GROUPS, GROUP, NB), F32),
-            vmem((GROUPS, NZ - 1, 8, NB), F32),
-            vmem((GROUPS, 8, NB), F32),
-            vmem((GROUPS, NX - 1, 8, NB), F32),
-            vmem((GROUPS, 8, NB), F32),
-            vmem((GROUPS, NZ - 1, 8, NB), F32),
+            vmem((UNITS, GROUP, NB), F32),
+            vmem((UNITS, NX - 1, 16, NB), F32),
+            vmem((UNITS, 16, NB), F32),
+            vmem((UNITS, NZ - 1, 16, NB), F32),
+            vmem((UNITS, 16, NB), F32),
+            vmem((UNITS, NX - 1, 16, NB), F32),
             vmem((2 * NB, NB), F32),
             vmem((3, 8, NB), F32),
             vmem((3, NZ - 1, 8, NB), F32),
@@ -547,7 +608,8 @@
             dma((2, CHUNKS)),
             dma((2, CHUNKS)),
             dma((2, CHUNKS)),
-            *[dma((GROUPS,))] * 6,
+            dma((2, CHUNKS - DIRECT)),
+            *[dma((UNITS,))] * 6,
             *[dma((3,))] * 6,
             *[dma((1,))] * 4,
         ],

time: 85.4 us -> 80 us (0.937)
  the two profiles are of different devices: /device:TPU:8 before, /device:TPU:9 now
where the time goes in v2:
time: 80 us; the launch traced here: 79.3 us
  Pallas kernels  76.7 us (96%)
  local copies, waits for them, and re-layouts  2.62 us (3%)
    pallas_call x1, Pallas kernels, local(): pl.pallas_call(kernel, out_shape=jax.ShapeDtypeStruct((ROWS, NB), F32), i...  76.7 us
    unnamed x3, local copies, waits for them, and re-layouts  2.62 us

profile of v2, /device:TPU:9, one launch (start us, length us, event | category | flops | bytes accessed | tf_op | source)
XLA Modules:
  0.0 79.3 jit_solution(13656642547742566153)
XLA Ops:
  0.0 0.0 copy-start
  0.0 0.9 %copy-done = f32[1,256,256]{2,1,0:T(8,128)S(1)} copy-done((f32[1,256,256]{2,1,0:T(8,128)S(1)}, f32[1,256,256]{2,1,0:T(8,128)}, u32[]{:S(2)}) %copy-start) | copy-done | bytes 262168
  1.0 76.7 %shard_map.37 = f32[3072,256]{1,0:T(8,128)S(1)} custom-call(f32[3072,256]{1,0:T(8,128)} %e_hbm.1, f32[3072,256]{1,0:T(8,128)} %v_hbm.1, f32[1,256,256]{2,1,0:T(8,128)S(1)} %copy-done), custom_call_target="tpu_custom_call" | custom-call | tf_op jit(solution)/shard_map/pallas_call | solution.py:575
  77.7 1.7 %copy.5 = f32[3072,256]{1,0:T(8,128)} copy(f32[3072,256]{1,0:T(8,128)S(1)} %shard_map.37) | data formatting | bytes 6291456
Async XLA Ops:
  0.0 0.9 %copy-start = (f32[1,256,256]{2,1,0:T(8,128)S(1)}, f32[1,256,256]{2,1,0:T(8,128)}, u32[]{:S(2)}) copy-start(f32[1,256,256]{2,1,0:T(8,128)} %f_hbm.1) | copy-start | bytes 786436

commit v3 on v2

--- a/solution.py
+++ b/solution.py
@@ -43,13 +43,13 @@
 
 
 def kernel(
-    e_hbm, v_hbm, f_hbm, out_hbm,
+    e_hbm, v_hbm, f_hbm, out,
     e, raw, eh, el, vt, vn,
     wloc, x_land, zs, z_land, red, ag_land, wfull,
     ms, mz_land, mz, mx_land, mats,
     gacc, gloc, gz_land, gq, gx_land,
     s_stack, s_low,
-    load_sem, out_sem, recv, send, sib,
+    known, load_sem, recv, send, sib,
     direct, x_s, x_r, z_s, z_r, ag_s, ag_r,
     ms_s, ms_r, mz_s, mz_r, mx_s, mx_r,
     gz_s, gz_r, gx_s, gx_r,
@@ -100,13 +100,11 @@
     def greet(device):
         pl.semaphore_signal(barrier, inc=1, device_id=device, device_id_type=MESH)
 
-    for d in range(1, NZ):
-        greet(z_peer(d))
-    for d in range(1, NX):
-        greet(x_peer(d))
-    greet(ring(y, 1 - core))
-
-    @pl.when(jnp.logical_not(at_root))
+    neighbours = (z_peer(1), z_peer(NZ - 1), x_peer(1), x_peer(NX - 1), ring(y, 1 - core))
+    for device in neighbours:
+        greet(device)
+
+    @pl.when(y % 2 == 1)
     def _():
         greet(ring(0, 0))
         greet(ring(0, 1))
@@ -133,11 +131,26 @@
         load_f.wait()
         transpose_in(0)
 
-    pl.semaphore_wait(barrier, (NZ - 1) + (NX - 1) + jnp.where(at_root, 7, jnp.where(last, 1, 2)))
+    pl.semaphore_wait(barrier, len(neighbours) + jnp.where(at_root, 4, jnp.where(last, 0, 1)))
+
+    def tell(n):
+        pl.semaphore_signal(known.at[n, 0], inc=1, device_id=z_peer(1), device_id_type=MESH)
+        pl.semaphore_signal(known.at[n, 1], inc=1, device_id=z_peer(NZ - 1), device_id_type=MESH)
+        if n == 0:
+            pl.semaphore_signal(known.at[n, 2], inc=1, device_id=x_peer(1), device_id_type=MESH)
+
+    def hear(n):
+        for which in range(3 if n == 0 else 2):
+            pl.semaphore_wait(known.at[n, which], 1)
+
+    tell(0)
 
     def spread(m):
-        for d in range(1, NCOL):
-            yield remote(ms.at[m], ms.at[m], ms_s.at[m], ms_r.at[m], (row, lax.rem(col + d, NCOL)))
+        for device in (ring(0, 1 - core), ring(1, 0), ring(1, 1), ring(3, 0), ring(3, 1)):
+            yield remote(ms.at[m], ms.at[m], ms_s.at[m], ms_r.at[m], device)
+
+    def spread_on(m):
+        return remote(ms.at[m], ms.at[m], ms_s.at[m], ms_r.at[m], ring(2, core))
 
     for m in range(2):
 
@@ -326,6 +339,10 @@
         def _():
             whole(ms.at[m], ms_s.at[m], ms_r.at[m]).wait_recv()
 
+        @pl.when(first)
+        def _():
+            spread_on(m).start()
+
         for copy in m_to_z(m):
             copy.start()
 
@@ -420,6 +437,11 @@
         def _():
             when(at_root, transpose_in, 1)
 
+        @pl.when(i == 1)
+        def _():
+            hear(1)
+            tell(2)
+
         @pl.when(done >= 0)
         def _():
             other_half(done, 0, TICKS)
@@ -438,6 +460,13 @@
         when(i == 0, split_field)
         when(done >= 1, lambda: transpose_out((done - 1) // 2, (done - 1) % 2))
         when(i < GROUPS, ticks, i, 3, 4)
+
+        @pl.when(i == 0)
+        def _():
+            hear(0)
+            tell(1)
+
+        when(i == 1, hear, 2)
 
         @pl.when(done == 1)
         def _():
@@ -465,22 +494,70 @@
     other_half(GROUPS - 1, TICKS // 2, TICKS)
     project(GROUPS)
 
+    def left(u):
+        whole(part(x_land, u), x_s.at[u], x_r.at[u]).wait_send()
+        whole(part(z_land, u), z_s.at[u], z_r.at[u]).wait_send()
+        whole(part(ag_land, u), ag_s.at[u], ag_r.at[u]).wait_send()
+
+    def matrices_left():
+        for m in range(3):
+            whole(mz_land.at[m], mz_s.at[m], mz_r.at[m]).wait_send()
+            whole(mx_land.at[m], mx_s.at[m], mx_r.at[m]).wait_send()
+
+            @pl.when(at_root & ((core == 1) if m == 0 else (core == 0)))
+            def _():
+                whole(mz_land.at[m, pl.ds(0, 5)], ms_s.at[m], ms_r.at[m]).wait_send()
+
+            @pl.when(first)
+            def _():
+                spread_on(m).wait_send()
+
+        @pl.when(overlap_here)
+        def _():
+            whole(gz_land, gz_s.at[0], gz_r.at[0]).wait_send()
+            whole(gx_land, gx_s.at[0], gx_r.at[0]).wait_send()
+
+    def stream_left():
+        def drain(k, _):
+            @pl.when(jnp.logical_not(at_root))
+            def _():
+                @pl.when(relays(k))
+                def _():
+                    ahead_send(k).wait_send()
+
+                pass_on(k).wait_send()
+
+            @pl.when(at_root & ((core == 1) == (k < CHUNKS // 2)))
+            def _():
+                for h in range(2):
+                    sib_send(k, h).wait_send()
+
+                    @pl.when(k % (CHUNKS // 2) >= CHUNKS // 2 - DEPTH)
+                    def _():
+                        ring_send(k, h).wait_send()
+
+                    @pl.when(k >= DIRECT)
+                    def _():
+                        direct_send(k, h).wait_send()
+
+            return 0
+
+        lax.fori_loop(0, CHUNKS, drain, 0)
+
     def set_s(j, value):
         high, low = split(value)
         s_stack[j, :TILE] = high
         s_stack[j, TILE:] = high
         s_low[j] = low
 
-    def update(tiles, finish):
+    def update(tiles, target):
         def body(n, _):
             rows = pl.ds(pl.multiple_of(n * 512, 512), 512)
             total = e[rows, :]
             for j in tiles:
                 part = vn[j, rows, :]
                 total -= dot(part, s_stack[j]) + dot(part[:, :TILE], s_low[j])
-            e[rows, :] = total
-            if finish:
-                pltpu.make_async_copy(e.at[rows], out_hbm.at[rows], out_sem.at[n]).start()
+            target[rows, :] = total
             return 0
 
         lax.fori_loop(0, ROWS // 512, body, 0)
@@ -501,82 +578,35 @@
     set_s(0, first_s[:TILE])
     set_s(1, first_s[TILE:])
     sum_z(6)
-    update((0, 1), False)
+    stream_left()
     sum_z(7)
     sum_z(8)
+    update((0, 1), e)
     gather(4)
     gather(5)
     m_end(2)
     correction = product(mats[2], first_s)
     upper = wfull[NB + TILE :, :] - correction[TILE:]
     set_s(2, product(mats[1, TILE:, TILE:], upper))
-    update((2,), False)
+    update((2,), e)
+    matrices_left()
+    for u in range(UNITS):
+        left(u)
     gather(6)
     gather(7)
     gather(8)
     lower = wfull[NB : NB + TILE, :] - correction[:TILE]
     set_s(3, product(mats[1, :TILE, :], jnp.concatenate([lower, upper], axis=0)))
-    update((3,), True)
-
-    for u in range(UNITS):
-        whole(part(x_land, u), x_s.at[u], x_r.at[u]).wait_send()
-        whole(part(z_land, u), z_s.at[u], z_r.at[u]).wait_send()
-        whole(part(ag_land, u), ag_s.at[u], ag_r.at[u]).wait_send()
-    for m in range(3):
-        whole(mz_land.at[m], mz_s.at[m], mz_r.at[m]).wait_send()
-        whole(mx_land.at[m], mx_s.at[m], mx_r.at[m]).wait_send()
-
-        @pl.when(at_root & ((core == 1) if m == 0 else (core == 0)))
-        def _():
-            whole(mz_land.at[m], ms_s.at[m], ms_r.at[m]).wait_send()
-
-    @pl.when(overlap_here)
-    def _():
-        whole(gz_land, gz_s.at[0], gz_r.at[0]).wait_send()
-        whole(gx_land, gx_s.at[0], gx_r.at[0]).wait_send()
-
-    def drain(k, _):
-        @pl.when(jnp.logical_not(at_root))
-        def _():
-            @pl.when(relays(k))
-            def _():
-                ahead_send(k).wait_send()
-
-            pass_on(k).wait_send()
-
-        @pl.when(at_root & ((core == 1) == (k < CHUNKS // 2)))
-        def _():
-            for h in range(2):
-                sib_send(k, h).wait_send()
-
-                @pl.when(k % (CHUNKS // 2) >= CHUNKS // 2 - DEPTH)
-                def _():
-                    ring_send(k, h).wait_send()
-
-                @pl.when(k >= DIRECT)
-                def _():
-                    direct_send(k, h).wait_send()
-
-        return 0
-
-    lax.fori_loop(0, CHUNKS, drain, 0)
-
-    def finish(n, _):
-        rows = pl.ds(pl.multiple_of(n * 512, 512), 512)
-        pltpu.make_async_copy(e.at[rows], out_hbm.at[rows], out_sem.at[n]).wait()
-        return 0
-
-    lax.fori_loop(0, ROWS // 512, finish, 0)
+    update((3,), out)
 
 
 def local(eigvecs, reflectors, factors):
     vmem, dma = pltpu.VMEM, pltpu.SemaphoreType.DMA
-    anywhere = pl.BlockSpec(memory_space=pl.ANY)
     return pl.pallas_call(
         kernel,
         out_shape=jax.ShapeDtypeStruct((ROWS, NB), F32),
         in_specs=[pl.BlockSpec(memory_space=pltpu.HBM)] * 3,
-        out_specs=anywhere,
+        out_specs=pl.BlockSpec(memory_space=pltpu.VMEM),
         scratch_shapes=[
             vmem((ROWS, NB), F32),
             vmem((ROWS, NB), F32),
@@ -603,8 +633,8 @@
             vmem((NX - 1, 8, NB), F32),
             vmem((4, NB, NB), BF16),
             vmem((4, TILE, NB), BF16),
+            pltpu.SemaphoreType.REGULAR((3, 3)),
             dma((3,)),
-            dma((ROWS // 512,)),
             dma((2, CHUNKS)),
             dma((2, CHUNKS)),
             dma((2, CHUNKS)),

time: 80 us -> 84.6 us (1.057)
  Pallas kernels: 76.7 us -> 81.4 us
    pallas_call x1, Pallas kernels: 76.7 us -> 81.4 us  [local(): pl.pallas_call(kernel, out_shape=jax.ShapeDtypeStruct((ROWS, NB), F32), i...]
where the time goes in v3:
time: 84.6 us; the launch traced here: 84 us
  Pallas kernels  81.4 us (96%)
  local copies, waits for them, and re-layouts  2.62 us (3%)
    pallas_call x1, Pallas kernels, local(): pl.pallas_call(kernel, out_shape=jax.ShapeDtypeStruct((ROWS, NB), F32), i...  81.4 us
    unnamed x3, local copies, waits for them, and re-layouts  2.62 us

profile of v3, /device:TPU:9, one launch (start us, length us, event | category | flops | bytes accessed | tf_op | source)
XLA Modules:
  0.0 84.0 jit_solution(4240374805233068160)
XLA Ops:
  0.0 0.0 copy-start
  0.0 0.9 %copy-done = f32[1,256,256]{2,1,0:T(8,128)S(1)} copy-done((f32[1,256,256]{2,1,0:T(8,128)S(1)}, f32[1,256,256]{2,1,0:T(8,128)}, u32[]{:S(2)}) %copy-start) | copy-done | bytes 262168
  1.0 81.4 %shard_map.37 = f32[3072,256]{1,0:T(8,128)S(1)} custom-call(f32[3072,256]{1,0:T(8,128)} %e_hbm.1, f32[3072,256]{1,0:T(8,128)} %v_hbm.1, f32[1,256,256]{2,1,0:T(8,128)S(1)} %copy-done), custom_call_target="tpu_custom_call" | custom-call | tf_op jit(solution)/shard_map/pallas_call | solution.py:605
  82.4 1.7 %copy.5 = f32[3072,256]{1,0:T(8,128)} copy(f32[3072,256]{1,0:T(8,128)S(1)} %shard_map.37) | data formatting | bytes 6291456
Async XLA Ops:
  0.0 0.9 %copy-start = (f32[1,256,256]{2,1,0:T(8,128)S(1)}, f32[1,256,256]{2,1,0:T(8,128)}, u32[]{:S(2)}) copy-start(f32[1,256,256]{2,1,0:T(8,128)} %f_hbm.1) | copy-start | bytes 786436

commit v4 on v3

--- a/solution.py
+++ b/solution.py
@@ -48,8 +48,7 @@
     wloc, x_land, zs, z_land, red, ag_land, wfull,
     ms, mz_land, mz, mx_land, mats,
     gacc, gloc, gz_land, gq, gx_land,
-    s_stack, s_low,
-    known, load_sem, recv, send, sib,
+    known, load_sem, recv, send, sib, passed,
     direct, x_s, x_r, z_s, z_r, ag_s, ag_r,
     ms_s, ms_r, mz_s, mz_r, mx_s, mx_r,
     gz_s, gz_r, gx_s, gx_r,
@@ -73,7 +72,7 @@
     last = ((core == 1) & (y == 3)) | ((core == 0) & (y == 1))
     ahead = jnp.where(core == 1, y + 1, y - 1)
     behind = jnp.where(core == 1, y - 1, y + 1)
-    lag = jnp.where(first, 4, jnp.where(y == 2, 2, 1))
+    lag = jnp.where(first, 3, jnp.where(y == 2, 2, 1))
     mine = 1 - core
     rank = x * NZ + z
 
@@ -114,16 +113,10 @@
         greet(ring(behind, core))
 
     def transpose_in(ct):
-        panel = 1 - core
-
-        def body(rt, _):
-            start = pl.multiple_of(rt * TILE, TILE)
-            for h in range(2):
-                block = raw[pl.ds(pl.multiple_of(h * HALF + start, TILE), TILE), ct * TILE : (ct + 1) * TILE]
-                vt[panel, h, ct * TILE : (ct + 1) * TILE, pl.ds(start, TILE)] = block.T
-            return 0
-
-        lax.fori_loop(0, HALF // TILE, body, 0)
+        columns = slice(ct * TILE, (ct + 1) * TILE)
+        for start in range(0, ROWS, TILE):
+            lanes = slice(start % HALF, start % HALF + TILE)
+            vt[1 - core, start // HALF, columns, lanes] = raw[start : start + TILE, columns].T
 
     @pl.when(at_root)
     def _():
@@ -181,13 +174,13 @@
         return jnp.logical_not(last | ((y == 2) & (k >= DIRECT)))
 
     def sib_send(k, h):
-        return piece(k, h, sib.at[h, k], ring(y, 1 - core))
+        return piece(k, h, sib.at[0], ring(y, 1 - core))
 
     def ahead_send(k):
-        return piece(k, mine, send.at[0, k], ring(ahead, core))
+        return piece(k, mine, passed.at[k // (CHUNKS // 2)], ring(ahead, core))
 
     def pass_on(k):
-        return piece(k, mine, sib.at[0, k], ring(y, 1 - core))
+        return piece(k, mine, sib.at[0], ring(y, 1 - core))
 
     def arrived(k, h):
         piece(k, h, send.at[0, k], ring(y, 1 - core)).wait_recv()
@@ -309,20 +302,28 @@
             origin = lax.rem(x + NX - d, NX)
             wfull[pl.ds(pl.multiple_of(base + origin * n, 8), n), :] = ag_land[u, d - 1, :n]
 
-    def tile_column(j):
-        return pl.multiple_of(jnp.where((j == 1) | (j == 2), TILE, 0), TILE)
-
-    def transpose_out(j, h):
-        def body(rt, _):
-            start = pl.multiple_of(rt * TILE, TILE)
-            block = vt[j // 2, h, pl.ds(tile_column(j), TILE), pl.ds(start, TILE)]
-            high, low = split(block.T)
+    def transpose_first(j, h):
+        columns = pl.ds(pl.multiple_of(j * TILE, TILE), TILE)
+        for start in range(0, HALF, TILE):
+            high, low = split(vt[0, h, columns, start : start + TILE].T)
             rows = pl.ds(pl.multiple_of(h * HALF + start, TILE), TILE)
-            vn[j, rows, :TILE] = high
-            vn[j, rows, TILE:] = low
-            return 0
-
-        lax.fori_loop(0, HALF // TILE, body, 0)
+            vn[0, rows, columns] = high
+            vn[1, rows, columns] = low
+
+    def transpose_upper(h):
+        for start in range(0, HALF, TILE):
+            high, low = split(vt[1, h, TILE:, start : start + TILE].T)
+            rows = pl.ds(pl.multiple_of(h * HALF + start, TILE), TILE)
+            vn[2, rows, :TILE] = high
+            vn[2, rows, TILE:] = low
+
+    def transpose_quarter(q):
+        for start in range(0, ROWS, TILE):
+            lanes = slice(start % HALF, start % HALF + TILE)
+            high, low = split(vt[1, start // HALF, q * 64 : (q + 1) * 64, lanes])
+            both = jnp.concatenate([high.astype(F32), low.astype(F32)], axis=0).T.astype(BF16)
+            vn[3 + q, start : start + TILE, :TILE] = both
+            vn[3 + q, start : start + TILE, TILE:] = both
 
     def m_to_z(m):
         for d in range(1, NZ):
@@ -335,16 +336,16 @@
     def m_begin(m):
         is_source = at_root & ((core == 1) if m == 0 else (core == 0))
 
-        @pl.when(jnp.logical_not(is_source))
+        @pl.when(jnp.logical_not(is_source | first))
         def _():
             whole(ms.at[m], ms_s.at[m], ms_r.at[m]).wait_recv()
 
-        @pl.when(first)
-        def _():
-            spread_on(m).start()
-
         for copy in m_to_z(m):
             copy.start()
+
+    def m_forward(m):
+        whole(ms.at[m], ms_s.at[m], ms_r.at[m]).wait_recv()
+        spread_on(m).start()
 
     def m_middle(m):
         whole(mz_land.at[m], mz_s.at[m], mz_r.at[m]).wait_recv()
@@ -373,17 +374,12 @@
             yield remote(gq.at[lax.rem(x + d, NX)], gx_land.at[d - 1], gx_s.at[0], gx_r.at[0], x_peer(d))
 
     def overlap_begin():
-        gacc[...] = jnp.zeros_like(gacc)
-
-        def body(n, _):
-            h, part = n // 3, n % 3
-            lanes = pl.ds(pl.multiple_of(part * 512, 512), 512)
-            ah, al = split(vt[1, h, :, lanes])
-            bh, bl = split(vt[0, h, :, lanes])
-            gacc[...] += dot_nt(ah, bh) + dot_nt(ah, bl) + dot_nt(al, bh)
-            return 0
-
-        lax.fori_loop(0, 6, body, 0)
+        total = jnp.zeros((NB, NB), F32)
+        for h in range(2):
+            ah, al = split(vt[1, h])
+            bh, bl = split(vt[0, h])
+            total += dot_nt(ah, bh) + dot_nt(ah, bl) + dot_nt(al, bh)
+        gacc[...] = total
         for zz in range(NZ):
             for xx in range(NX):
                 gloc[zz, xx] = gacc[xx * 64 + zz * 8 : xx * 64 + zz * 8 + 8, :]
@@ -429,6 +425,10 @@
             for t in range(begin, end):
                 arrived(done * TICKS + t, core)
 
+    def factors_end():
+        m_end(0)
+        m_end(1)
+
     def step(i, _):
         done = i - lag
         when(i < GROUPS, ticks, i, 0, 1)
@@ -448,43 +448,63 @@
             project(done)
 
         when(i < GROUPS, ticks, i, 1, 2)
-        when(done >= 1, sum_x, done - 1)
-        when(done >= 3, sum_z, done - 3)
-        when(i < GROUPS, ticks, i, 2, 3)
-
-        @pl.when((i == GROUPS - 1) & last)
-        def _():
-            other_half(GROUPS - 1, 0, TICKS // 2)
-            project(GROUPS - 1)
-
-        when(i == 0, split_field)
-        when(done >= 1, lambda: transpose_out((done - 1) // 2, (done - 1) % 2))
-        when(i < GROUPS, ticks, i, 3, 4)
-
-        @pl.when(i == 0)
-        def _():
-            hear(0)
-            tell(1)
-
-        when(i == 1, hear, 2)
-
-        @pl.when(done == 1)
-        def _():
-            m_begin(0)
-            m_begin(1)
-
-        @pl.when(done == 3)
-        def _():
-            m_middle(0)
-            m_middle(1)
-
         when(overlap_here & (i == 4), overlap_begin)
         when(overlap_here & (i == 6), overlap_middle)
         when(overlap_here & (i == 7), overlap_end)
-        when(done == 6, m_begin, 2)
+        when(first & (i == 7), m_forward, 2)
+        when(i == 7, m_begin, 2)
+        when((done >= 1) & (i < GROUPS), sum_x, done - 1)
+        when((done >= 3) & (i < GROUPS), sum_z, done - 3)
+        when(i < GROUPS, ticks, i, 2, 3)
+
+        @pl.when((i == GROUPS - 1) & last)
+        def _():
+            other_half(GROUPS - 1, 0, TICKS // 2)
+            project(GROUPS - 1)
+
+        when(i == 0, split_field)
+        when((done >= 1) & (done <= 4), lambda: transpose_first((done - 1) // 2, (done - 1) % 2))
+        when((done == 5) | (done == 6), lambda: transpose_upper(done - 5))
+        when(i < GROUPS, ticks, i, 3, 4)
+
+        @pl.when(i == 0)
+        def _():
+            hear(0)
+            tell(1)
+
+        @pl.when(i == 1)
+        def _():
+            hear(2)
+
+            @pl.when(first)
+            def _():
+                m_forward(0)
+                m_forward(1)
+
+
+        @pl.when(done == 1)
+        def _():
+            m_begin(0)
+            m_begin(1)
+
+        @pl.when(done == 3)
+        def _():
+            m_middle(0)
+            m_middle(1)
+
+        when(done == 5, factors_end)
         return 0
 
     lax.fori_loop(0, GROUPS - 1 + lag, step, 0)
+
+    def sums(action, begin, end):
+        def body(u, _):
+            action(u)
+            return 0
+
+        lax.fori_loop(begin, end, body, 0)
+
+    sums(sum_x, GROUPS - 1 - lag, GROUPS - 2)
 
     @pl.when(jnp.logical_not(last))
     def _():
@@ -518,86 +538,78 @@
             whole(gx_land, gx_s.at[0], gx_r.at[0]).wait_send()
 
     def stream_left():
-        def drain(k, _):
-            @pl.when(jnp.logical_not(at_root))
-            def _():
-                @pl.when(relays(k))
-                def _():
-                    ahead_send(k).wait_send()
-
-                pass_on(k).wait_send()
-
-            @pl.when(at_root & ((core == 1) == (k < CHUNKS // 2)))
-            def _():
-                for h in range(2):
-                    sib_send(k, h).wait_send()
-
-                    @pl.when(k % (CHUNKS // 2) >= CHUNKS // 2 - DEPTH)
-                    def _():
-                        ring_send(k, h).wait_send()
-
-                    @pl.when(k >= DIRECT)
-                    def _():
-                        direct_send(k, h).wait_send()
-
-            return 0
-
-        lax.fori_loop(0, CHUNKS, drain, 0)
-
-    def set_s(j, value):
+        @pl.when(jnp.logical_not(at_root))
+        def _():
+            whole(vt.at[:, mine], sib.at[0], sib.at[0]).wait_send()
+
+            @pl.when(jnp.logical_not(last))
+            def _():
+                whole(vt.at[0, mine], passed.at[0], sib.at[0]).wait_send()
+
+            @pl.when(first)
+            def _():
+                whole(vt.at[1, mine], passed.at[1], sib.at[0]).wait_send()
+
+            @pl.when(y == 2)
+            def _():
+                sent = NB - (CHUNKS - DIRECT) * TICK
+                whole(vt.at[1, mine, pl.ds(0, sent), :], passed.at[1], sib.at[0]).wait_send()
+
+        @pl.when(at_root)
+        def _():
+            whole(vt.at[1 - core], sib.at[0], sib.at[0]).wait_send()
+            base = (1 - core) * (CHUNKS // 2)
+            for h in range(2):
+                for t in range(CHUNKS // 2 - DEPTH, CHUNKS // 2):
+                    ring_send(base + t, h).wait_send()
+
+        @pl.when(at_root & (core == 0))
+        def _():
+            for h in range(2):
+                for k in range(DIRECT, CHUNKS):
+                    direct_send(k, h).wait_send()
+
+    def quarter(q, value):
         high, low = split(value)
-        s_stack[j, :TILE] = high
-        s_stack[j, TILE:] = high
-        s_low[j] = low
-
-    def update(tiles, target):
-        def body(n, _):
-            rows = pl.ds(pl.multiple_of(n * 512, 512), 512)
-            total = e[rows, :]
-            for j in tiles:
-                part = vn[j, rows, :]
-                total -= dot(part, s_stack[j]) + dot(part[:, :TILE], s_low[j])
-            target[rows, :] = total
-            return 0
-
-        lax.fori_loop(0, ROWS // 512, body, 0)
-
+        stacked = jnp.concatenate([high, high, low, jnp.zeros_like(low)], axis=0)
+        return dot(vn[3 + q], stacked)
+
+    sums(sum_z, GROUPS - 3 - lag, GROUPS - 4)
     sum_x(6)
     sum_z(4)
-    transpose_out(3, 0)
-    sum_x(7)
-    sum_x(8)
-    sum_z(5)
-    m_end(0)
-    m_end(1)
-    transpose_out(3, 1)
     m_middle(2)
     for u in range(4):
         gather(u)
     first_s = product(mats[0], wfull[:NB, :])
-    set_s(0, first_s[:TILE])
-    set_s(1, first_s[TILE:])
+    high, low = split(first_s)
+    e[...] -= dot(vn[0], high) + dot(vn[0], low) + dot(vn[1], high)
+    sum_x(7)
+    transpose_quarter(1)
+    sum_x(8)
+    transpose_quarter(0)
+    sum_z(5)
+    stream_left()
+    gather(4)
+    m_end(2)
+    correction = product(mats[2], first_s)
     sum_z(6)
-    stream_left()
+    gather(5)
+    upper = wfull[NB + TILE :, :] - correction[TILE:]
+    high, low = split(product(mats[1, TILE:, TILE:], upper))
     sum_z(7)
     sum_z(8)
-    update((0, 1), e)
-    gather(4)
-    gather(5)
-    m_end(2)
-    correction = product(mats[2], first_s)
-    upper = wfull[NB + TILE :, :] - correction[TILE:]
-    set_s(2, product(mats[1, TILE:, TILE:], upper))
-    update((2,), e)
+    e[...] -= dot(vn[2], jnp.concatenate([high, high], axis=0)) + dot(vn[2, :, :TILE], low)
+    gather(6)
+    next_u = wfull[NB + 64 : NB + TILE, :] - correction[64:TILE]
+    known_u = jnp.concatenate([jnp.zeros_like(next_u), next_u, upper], axis=0)
+    e[...] -= quarter(1, product(mats[1, 64:TILE, :], known_u))
     matrices_left()
     for u in range(UNITS):
         left(u)
-    gather(6)
     gather(7)
     gather(8)
-    lower = wfull[NB : NB + TILE, :] - correction[:TILE]
-    set_s(3, product(mats[1, :TILE, :], jnp.concatenate([lower, upper], axis=0)))
-    update((3,), out)
+    last_u = wfull[NB : NB + 64, :] - correction[:64]
+    out[...] = e[...] - quarter(0, product(mats[1, :64, :], jnp.concatenate([last_u, next_u, upper], axis=0)))
 
 
 def local(eigvecs, reflectors, factors):
@@ -613,7 +625,7 @@
             vmem((ROWS, NB), BF16),
             vmem((ROWS, NB), BF16),
             vmem((2, 2, NB, HALF), F32),
-            vmem((4, ROWS, NB), BF16),
+            vmem((5, ROWS, NB), BF16),
             vmem((UNITS, GROUP, NB), F32),
             vmem((UNITS, NX - 1, 16, NB), F32),
             vmem((UNITS, 16, NB), F32),
@@ -631,13 +643,12 @@
             vmem((NZ - 1, NX, 8, NB), F32),
             vmem((NX, 8, NB), F32),
             vmem((NX - 1, 8, NB), F32),
-            vmem((4, NB, NB), BF16),
-            vmem((4, TILE, NB), BF16),
             pltpu.SemaphoreType.REGULAR((3, 3)),
             dma((3,)),
             dma((2, CHUNKS)),
             dma((2, CHUNKS)),
-            dma((2, CHUNKS)),
+            dma((1,)),
+            dma((2,)),
             dma((2, CHUNKS - DIRECT)),
             *[dma((UNITS,))] * 6,
             *[dma((3,))] * 6,

time: 84.6 us -> 75.3 us (0.89)
  Pallas kernels: 81.4 us -> 72.6 us
    pallas_call x1, Pallas kernels: 81.4 us -> 72.6 us  [local(): pl.pallas_call(kernel, out_shape=jax.ShapeDtypeStruct((ROWS, NB), F32), i...]
where the time goes in v4:
time: 75.3 us; the launch traced here: 75.2 us
  Pallas kernels  72.6 us (96%)
  local copies, waits for them, and re-layouts  2.62 us (3%)
    pallas_call x1, Pallas kernels, local(): pl.pallas_call(kernel, out_shape=jax.ShapeDtypeStruct((ROWS, NB), F32), i...  72.6 us
    unnamed x3, local copies, waits for them, and re-layouts  2.62 us

profile of v4, /device:TPU:9, one launch (start us, length us, event | category | flops | bytes accessed | tf_op | source)
XLA Modules:
  0.0 75.2 jit_solution(10833502371366080265)
XLA Ops:
  0.0 0.0 copy-start
  0.0 0.9 %copy-done = f32[1,256,256]{2,1,0:T(8,128)S(1)} copy-done((f32[1,256,256]{2,1,0:T(8,128)S(1)}, f32[1,256,256]{2,1,0:T(8,128)}, u32[]{:S(2)}) %copy-start) | copy-done | bytes 262168
  1.0 72.6 %shard_map.37 = f32[3072,256]{1,0:T(8,128)S(1)} custom-call(f32[3072,256]{1,0:T(8,128)} %e_hbm.1, f32[3072,256]{1,0:T(8,128)} %v_hbm.1, f32[1,256,256]{2,1,0:T(8,128)S(1)} %copy-done), custom_call_target="tpu_custom_call" | custom-call | tf_op jit(solution)/shard_map/pallas_call | solution.py:617
  73.6 1.7 %copy.5 = f32[3072,256]{1,0:T(8,128)} copy(f32[3072,256]{1,0:T(8,128)S(1)} %shard_map.37) | data formatting | bytes 6291456
Async XLA Ops:
  0.0 0.9 %copy-start = (f32[1,256,256]{2,1,0:T(8,128)S(1)}, f32[1,256,256]{2,1,0:T(8,128)}, u32[]{:S(2)}) copy-start(f32[1,256,256]{2,1,0:T(8,128)} %f_hbm.1) | copy-start | bytes 786436

commit v5 on v4

--- a/solution.py
+++ b/solution.py
@@ -19,7 +19,7 @@
 CHUNKS = GROUPS * TICKS
 TILE = 128
 DEPTH = 3
-DIRECT = CHUNKS - 2
+DIRECT = CHUNKS - 4
 UNITS = GROUPS + 1
 
 
@@ -68,12 +68,13 @@
         return (z * NX + lax.rem(x + d, NX), col)
 
     at_root = y == 0
-    first = ((core == 1) & (y == 1)) | ((core == 0) & (y == 3))
-    last = ((core == 1) & (y == 3)) | ((core == 0) & (y == 1))
-    ahead = jnp.where(core == 1, y + 1, y - 1)
-    behind = jnp.where(core == 1, y - 1, y + 1)
-    lag = jnp.where(first, 3, jnp.where(y == 2, 2, 1))
-    mine = 1 - core
+    side = jnp.where(y == 3, 1 - core, core)
+    first = (core == 1) & (y % 2 == 1)
+    last = (core == 0) & (y % 2 == 1)
+    ahead = (jnp.where(side == 1, y + 1, y - 1), jnp.where(y == 1, core, 0))
+    behind = (jnp.where(side == 1, y - 1, y + 1), jnp.where(y == 1, 0, 1))
+    lag = jnp.where(first, 3, 1)
+    mine = 1 - side
     rank = x * NZ + z
 
     def remote(src, dst, send_sem, recv_sem, device):
@@ -110,7 +111,7 @@
 
     @pl.when(jnp.logical_not(at_root | first))
     def _():
-        greet(ring(behind, core))
+        greet(ring(*behind))
 
     def transpose_in(ct):
         columns = slice(ct * TILE, (ct + 1) * TILE)
@@ -143,7 +144,7 @@
             yield remote(ms.at[m], ms.at[m], ms_s.at[m], ms_r.at[m], device)
 
     def spread_on(m):
-        return remote(ms.at[m], ms.at[m], ms_s.at[m], ms_r.at[m], ring(2, core))
+        return remote(ms.at[m], ms.at[m], ms_s.at[m], ms_r.at[m], ring(*ahead))
 
     for m in range(2):
 
@@ -165,10 +166,10 @@
         return remote(ref, ref, send_sem, recv.at[h, k], device)
 
     def ring_send(k, h):
-        return piece(k, h, send.at[h, k], ring(jnp.where(h == 0, 1, 3), jnp.where(h == 0, 1, 0)))
+        return piece(k, h, send.at[h, k], ring(jnp.where(h == 0, 1, 3), 1))
 
     def direct_send(k, h):
-        return piece(k, h, direct.at[h, k - DIRECT], ring(jnp.where(h == 0, 3, 1), jnp.where(h == 0, 1, 0)))
+        return piece(k, h, direct.at[h, k - DIRECT], ring(jnp.where(h == 0, 3, 1), 0))
 
     def relays(k):
         return jnp.logical_not(last | ((y == 2) & (k >= DIRECT)))
@@ -177,7 +178,7 @@
         return piece(k, h, sib.at[0], ring(y, 1 - core))
 
     def ahead_send(k):
-        return piece(k, mine, passed.at[k // (CHUNKS // 2)], ring(ahead, core))
+        return piece(k, mine, passed.at[k // (CHUNKS // 2)], ring(*ahead))
 
     def pass_on(k):
         return piece(k, mine, sib.at[0], ring(y, 1 - core))
@@ -423,7 +424,7 @@
         @pl.when(jnp.logical_not(at_root))
         def _():
             for t in range(begin, end):
-                arrived(done * TICKS + t, core)
+                arrived(done * TICKS + t, 1 - mine)
 
     def factors_end():
         m_end(0)
@@ -453,8 +454,8 @@
         when(overlap_here & (i == 7), overlap_end)
         when(first & (i == 7), m_forward, 2)
         when(i == 7, m_begin, 2)
-        when((done >= 1) & (i < GROUPS), sum_x, done - 1)
-        when((done >= 3) & (i < GROUPS), sum_z, done - 3)
+        when((done >= 1) & (i <= GROUPS), sum_x, done - 1)
+        when((done >= 3) & (i <= GROUPS), sum_z, done - 3)
         when(i < GROUPS, ticks, i, 2, 3)
 
         @pl.when((i == GROUPS - 1) & last)
@@ -504,7 +505,8 @@
 
         lax.fori_loop(begin, end, body, 0)
 
-    sums(sum_x, GROUPS - 1 - lag, GROUPS - 2)
+    caught_up = jnp.where(first, 1, 0)
+    sums(sum_x, GROUPS - 1 - lag + caught_up, GROUPS - 2)
 
     @pl.when(jnp.logical_not(last))
     def _():
@@ -574,7 +576,7 @@
         stacked = jnp.concatenate([high, high, low, jnp.zeros_like(low)], axis=0)
         return dot(vn[3 + q], stacked)
 
-    sums(sum_z, GROUPS - 3 - lag, GROUPS - 4)
+    sums(sum_z, GROUPS - 3 - lag + caught_up, GROUPS - 4)
     sum_x(6)
     sum_z(4)
     m_middle(2)

time: 75.3 us -> 74.4 us (0.988)
  Pallas kernels: 72.6 us -> 71.7 us
    pallas_call x1, Pallas kernels: 72.6 us -> 71.7 us  [local(): pl.pallas_call(kernel, out_shape=jax.ShapeDtypeStruct((ROWS, NB), F32), i...]
where the time goes in v5:
time: 74.4 us; the launch traced here: 74.3 us
  Pallas kernels  71.7 us (96%)
  local copies, waits for them, and re-layouts  2.62 us (4%)
    pallas_call x1, Pallas kernels, local(): pl.pallas_call(kernel, out_shape=jax.ShapeDtypeStruct((ROWS, NB), F32), i...  71.7 us
    unnamed x3, local copies, waits for them, and re-layouts  2.62 us

profile of v5, /device:TPU:9, one launch (start us, length us, event | category | flops | bytes accessed | tf_op | source)
XLA Modules:
  0.0 74.3 jit_solution(8211834969064596955)
XLA Ops:
  0.0 0.0 copy-start
  0.0 0.9 %copy-done = f32[1,256,256]{2,1,0:T(8,128)S(1)} copy-done((f32[1,256,256]{2,1,0:T(8,128)S(1)}, f32[1,256,256]{2,1,0:T(8,128)}, u32[]{:S(2)}) %copy-start) | copy-done | bytes 262168
  1.0 71.7 %shard_map.37 = f32[3072,256]{1,0:T(8,128)S(1)} custom-call(f32[3072,256]{1,0:T(8,128)} %e_hbm.1, f32[3072,256]{1,0:T(8,128)} %v_hbm.1, f32[1,256,256]{2,1,0:T(8,128)S(1)} %copy-done), custom_call_target="tpu_custom_call" | custom-call | tf_op jit(solution)/shard_map/pallas_call | solution.py:619
  72.7 1.7 %copy.5 = f32[3072,256]{1,0:T(8,128)} copy(f32[3072,256]{1,0:T(8,128)S(1)} %shard_map.37) | data formatting | bytes 6291456
Async XLA Ops:
  0.0 0.9 %copy-start = (f32[1,256,256]{2,1,0:T(8,128)S(1)}, f32[1,256,256]{2,1,0:T(8,128)}, u32[]{:S(2)}) copy-start(f32[1,256,256]{2,1,0:T(8,128)} %f_hbm.1) | copy-start | bytes 786436

commit v6 on v5

--- a/solution.py
+++ b/solution.py
@@ -600,16 +600,16 @@
     high, low = split(product(mats[1, TILE:, TILE:], upper))
     sum_z(7)
     sum_z(8)
+    matrices_left()
     e[...] -= dot(vn[2], jnp.concatenate([high, high], axis=0)) + dot(vn[2, :, :TILE], low)
     gather(6)
     next_u = wfull[NB + 64 : NB + TILE, :] - correction[64:TILE]
     known_u = jnp.concatenate([jnp.zeros_like(next_u), next_u, upper], axis=0)
     e[...] -= quarter(1, product(mats[1, 64:TILE, :], known_u))
-    matrices_left()
+    gather(7)
+    gather(8)
     for u in range(UNITS):
         left(u)
-    gather(7)
-    gather(8)
     last_u = wfull[NB : NB + 64, :] - correction[:64]
     out[...] = e[...] - quarter(0, product(mats[1, :64, :], jnp.concatenate([last_u, next_u, upper], axis=0)))
 

time: 74.4 us -> 74.5 us (level)
  no operation moved by 1% of the time
where the time goes in v6:
time: 74.5 us; the launch traced here: 74.4 us
  Pallas kernels  71.7 us (96%)
  local copies, waits for them, and re-layouts  2.62 us (4%)
    pallas_call x1, Pallas kernels, local(): pl.pallas_call(kernel, out_shape=jax.ShapeDtypeStruct((ROWS, NB), F32), i...  71.7 us
    unnamed x3, local copies, waits for them, and re-layouts  2.62 us

profile of v6, /device:TPU:9, one launch (start us, length us, event | category | flops | bytes accessed | tf_op | source)
XLA Modules:
  0.0 74.4 jit_solution(5553608239619198551)
XLA Ops:
  0.0 0.0 copy-start
  0.0 0.9 %copy-done = f32[1,256,256]{2,1,0:T(8,128)S(1)} copy-done((f32[1,256,256]{2,1,0:T(8,128)S(1)}, f32[1,256,256]{2,1,0:T(8,128)}, u32[]{:S(2)}) %copy-start) | copy-done | bytes 262168
  1.0 71.7 %shard_map.37 = f32[3072,256]{1,0:T(8,128)S(1)} custom-call(f32[3072,256]{1,0:T(8,128)} %e_hbm.1, f32[3072,256]{1,0:T(8,128)} %v_hbm.1, f32[1,256,256]{2,1,0:T(8,128)S(1)} %copy-done), custom_call_target="tpu_custom_call" | custom-call | tf_op jit(solution)/shard_map/pallas_call | solution.py:619
  72.7 1.7 %copy.5 = f32[3072,256]{1,0:T(8,128)} copy(f32[3072,256]{1,0:T(8,128)S(1)} %shard_map.37) | data formatting | bytes 6291456
Async XLA Ops:
  0.0 0.9 %copy-start = (f32[1,256,256]{2,1,0:T(8,128)S(1)}, f32[1,256,256]{2,1,0:T(8,128)}, u32[]{:S(2)}) copy-start(f32[1,256,256]{2,1,0:T(8,128)} %f_hbm.1) | copy-start | bytes 786436
